TPU v7x, 32 devices: a whole 2x2x4 slice. The times are simulated.
32 devices in a mesh: bead: 8 (over y, x, core), atom: 4 (over z).
Axes of the slice: x: 2, y: 2, z: 4, core: 2. Of those that a mesh axis runs over, the one named last changes fastest.
Arguments:
- replica_point_fractions: float32 [128, 3, 6144], P('bead', None, 'atom'), may hold values from -1 to 2, as said below
- inverse_lattice_integers: int32 [3, 2048], P(None, 'bead'), may hold values from -10 to 10, as said below
- point_species_labels: int32 [6144], P('atom'), may hold values from 0 to 3
- species_electric_values: float32 [4], replicated, may hold values from -1 to 1
Outputs:
- bead_forces: float32 [128, 3, 6144], P('bead', None, 'atom')
Inputs may be any that keep to these rules, and one draw needn't show every extreme that they name: replica_point_fractions holds a site's position near a common centre in all beads, with its own offset in each bead. `inverse_lattice_integers`: its columns are distinct, none is all zeros, and none is the negative of another (the first nonzero entry of each column is positive).
All inputs are finite; a program needn't handle non-finite values.
Results may differ from a plain program's by a relative error of at most 0.0003.
Values sent between devices are 32-bit elements; how exact they have to be, the bound alone decides.
A program may use at most 64 MiB of HBM per device.

v0:
```python
import math

import jax
import jax.numpy as jnp
from jax import lax
from jax.sharding import PartitionSpec as P

CONTR = 8


TWO_PI = 2.0 * math.pi


def cycle_modes(length, count):
    index = jnp.arange(length, dtype=jnp.float32)
    rows = [jnp.ones((length,), jnp.float32) / math.sqrt(length)]
    for mode in range(1, count // 2):
        rows.append(math.sqrt(2.0 / length) * jnp.cos(TWO_PI * mode * index / length))
        rows.append(math.sqrt(2.0 / length) * jnp.sin(TWO_PI * mode * index / length))
    if length == count:
        rows.append(jnp.cos(math.pi * index) / math.sqrt(length))
    else:
        rows.append(math.sqrt(2.0 / length) * jnp.cos(TWO_PI * (count // 2) * index / length))
    return jnp.stack(rows)


def contraction_table(beads, contr):
    small = cycle_modes(contr, contr)
    big = cycle_modes(beads, contr)
    return math.sqrt(contr / beads) * jnp.dot(small.T, big, precision=lax.Precision.HIGHEST)


def fourier_mode_scaling(inverse_lattice_integers, number_points):
    fourier_mode_table = inverse_lattice_integers.astype(jnp.float32)
    square = jnp.sum(fourier_mode_table * fourier_mode_table, axis=0)
    return (fourier_mode_table, 4.0 * jnp.exp(-square / 100.0) / (square * number_points))


def phases(fourier_mode_table, position):
    return TWO_PI * jnp.dot(fourier_mode_table.T, position, precision=lax.Precision.HIGHEST)


def factor_parts(fourier_mode_table, charge, contracted):

    def structure(position):
        angle = phases(fourier_mode_table, position)
        return (
            jnp.dot(jnp.cos(angle), charge, precision=lax.Precision.HIGHEST),
            jnp.dot(jnp.sin(angle), charge, precision=lax.Precision.HIGHEST),
        )

    return lax.map(structure, contracted)


def force_parts(fourier_mode_table, fourier_mode_factor, charge, contracted, cos_fac, sin_fac):

    def forces(items):
        position, cfac, sfac = items
        angle = phases(fourier_mode_table, position)
        left = TWO_PI * fourier_mode_table * (fourier_mode_factor * cfac)[None, :]
        right = TWO_PI * fourier_mode_table * (fourier_mode_factor * sfac)[None, :]
        term = jnp.dot(left, jnp.sin(angle), precision=lax.Precision.HIGHEST) - jnp.dot(
            right, jnp.cos(angle), precision=lax.Precision.HIGHEST
        )
        return charge[None, :] * term

    return lax.map(forces, (contracted, cos_fac, sin_fac))


def local(
    replica_point_fractions, inverse_lattice_integers, point_species_labels, species_electric_values
):
    beads_local = replica_point_fractions.shape[0]
    beads = beads_local * lax.axis_size("bead")
    table = contraction_table(beads, CONTR)
    first_bead = lax.axis_index("bead") * beads_local
    local_table = lax.dynamic_slice_in_dim(table, first_bead, beads_local, 1)
    kinds = jnp.arange(species_electric_values.shape[0], dtype=jnp.int32)
    charge = jnp.sum(
        (point_species_labels[None, :] == kinds[:, None]).astype(jnp.float32)
        * species_electric_values[:, None],
        axis=0,
    )
    number_points = point_species_labels.shape[0] * lax.axis_size("atom")
    regrouped = lax.all_to_all(
        replica_point_fractions, "bead", split_axis=2, concat_axis=0, tiled=True
    )
    portion = jnp.einsum("jb,bxs->jxs", table, regrouped, precision=lax.Precision.HIGHEST)
    contracted = lax.all_gather(portion, "bead", axis=2, tiled=True)
    fourier_mode_table, fourier_mode_factor = fourier_mode_scaling(
        inverse_lattice_integers, number_points
    )
    cos_part, sin_part = factor_parts(fourier_mode_table, charge, contracted)
    cos_fac, sin_fac = lax.psum((cos_part, sin_part), "atom")
    partial_force = force_parts(
        fourier_mode_table, fourier_mode_factor, charge, contracted, cos_fac, sin_fac
    )
    summed = lax.psum(partial_force, "bead")
    return jnp.einsum("jb,jxs->bxs", local_table, summed, precision=lax.Precision.HIGHEST)


def solution(mesh):
    in_specs = (P("bead", None, "atom"), P(None, "bead"), P("atom"), P())
    out_specs = P("bead", None, "atom")
    return jax.shard_map(local, mesh=mesh, in_specs=in_specs, out_specs=out_specs, check_vma=False)
```

profile of v0, /device:TPU:0, one launch (start us, length us, event | category | flops | bytes accessed | tf_op | source)
XLA Modules:
  0.0 367.8 jit_solution(9848178092895601197)
XLA Ops:
  30.5 18.6 %all_gather.3 = f32[8,3,1536]{0,1,2:T(4,128)S(1)} all-gather(f32[8,3,192]{0,1,2:T(4,128)S(1)} %copy.24), channel_id=1, replica_groups=mesh['bead'=8,'atom'=4] {'bead'}, dimensions={2}, use_global_device_ids=true | all-gather | bytes 165888 | tf_op jit(solution)/shard_map/all_gather | solution.py:89
  50.3 105.9 %while.24 = (s32[]{:T(128)}, f32[8,256]{1,0:T(8,128)S(1)}, f32[8,256]{1,0:T(8,128)S(1)}, f32[8,3,1536]{2,1,0:T(4,128)S(1)}, f32[3,256]{1,0:T(4,128)S(1)}, /*inde...) while((s32[]{:T(128)}, f32[8,256]{1,0:T(8,128)S(1)}, f32[8,256]{1,0:T(8,128)S(1)}, ...), condition=%wide.wide.region_2.3_spmd, body=%wide.wide.region_1.0_spmd.sunk | while | flops 23986176 | bytes 4765801 | solution.py:52
  57.8 5.8 %fusion.74 = f32[1,256]{1,0:T(1,128)S(1)} fusion(f32[1536,1]{0,1:T(1,128)S(1)} %get-tuple-element.327, f32[1536,256]{1,0:T(8,128)S(1)} %convolution_multiply_fusion.7), kind=kOutput, calls=%fused_computation.1.clone.clone.1 | convolution fusion | flops 4718592 | bytes 1580032 | tf_op jit(solution)/shard_map/while/body/eval_jaxpr/dot_general | solution.py:49
  97.4 5.8 %fusion.74 = f32[1,256]{1,0:T(1,128)S(1)} fusion(f32[1536,1]{0,1:T(1,128)S(1)} %get-tuple-element.327, f32[1536,256]{1,0:T(8,128)S(1)} %convolution_multiply_fusion.7), kind=kOutput, calls=%fused_computation.1.clone.clone.1 | convolution fusion | flops 4718592 | bytes 1580032 | tf_op jit(solution)/shard_map/while/body/eval_jaxpr/dot_general | solution.py:49
  123.8 5.8 %fusion.74 = f32[1,256]{1,0:T(1,128)S(1)} fusion(f32[1536,1]{0,1:T(1,128)S(1)} %get-tuple-element.327, f32[1536,256]{1,0:T(8,128)S(1)} %convolution_multiply_fusion.7), kind=kOutput, calls=%fused_computation.1.clone.clone.1 | convolution fusion | flops 4718592 | bytes 1580032 | tf_op jit(solution)/shard_map/while/body/eval_jaxpr/dot_general | solution.py:49
  156.3 19.0 %all-reduce = (f32[8,256]{1,0:T(8,128)S(1)}, f32[8,256]{1,0:T(8,128)S(1)}) all-reduce(f32[8,256]{1,0:T(8,128)S(1)} %get-tuple-element.80, f32[8,256]{1,0:T(8,128)S(1)} %get-tuple-element.81), channel_id=1, replica_groups=mesh['bead'=8,'atom'=4] {'atom'}, use_global_device_ids=true, to_apply=%region_3.4 | all-reduce | flops 4096 | bytes 32768 | tf_op jit(solution)/shard_map/psum | solution.py:94
  175.3 134.2 %while.23 = (s32[]{:T(128)}, f32[8,3,1536]{2,0,1:T(8,128)}, f32[1536]{0:T(1024)}, f32[256]{0:T(256)S(1)}, f32[8,256]{1,0:T(8,128)S(1)}, /*index=5*/f32[3,256]{1,...) while((s32[]{:T(128)}, f32[8,3,1536]{2,0,1:T(8,128)}, ...), condition=%wide.region_7.8_spmd, body=%wide.region_6.7_spmd.sunk | while | flops 42872320 | bytes 4920461 | solution.py:67
  176.8 6.8 %fusion.65 = f32[3,1536]{1,0:T(4,128)S(1)} fusion(f32[1536,256]{1,0:T(8,128)S(1)} %convolution_multiply_fusion.6, f32[3,256]{1,0:T(4,128)S(1)} %get-tuple-element.355, f32[256]{0:T(256)S(1)} %bitcast.73), kind=kOutput, calls=%fused_computation.15.clone.1 | convolution fusion | flops 14156544 | bytes 1595392 | tf_op jit(solution)/shard_map/while/body/eval_jaxpr/dot_general | solution.py:62
  183.6 6.8 %fusion.66 = f32[1,3,1536]{2,1,0:T(4,128)S(1)} fusion(f32[3,1536]{1,0:T(4,128)S(1)} %fusion.65, f32[1536,256]{1,0:T(8,128)S(1)} %convolution_multiply_fusion.6, f32[1536]{0:T(1024)S(1)} %copy-done.1, f32[3,256]{1,0:T(4,128)S(1)} %get-tuple-element.355, f32[256]{0:T(256)S(1)} %bitcast.72), kind=kOutput, calls=%fused_computation.13.clone.1 | convolution fusion | flops 14165760 | bytes 1619968 | tf_op jit(solution)/shard_map/while/body/eval_jaxpr/dot_general | solution.py:62
  193.6 6.8 %fusion.65 = f32[3,1536]{1,0:T(4,128)S(1)} fusion(f32[1536,256]{1,0:T(8,128)S(1)} %convolution_multiply_fusion.6, f32[3,256]{1,0:T(4,128)S(1)} %get-tuple-element.355, f32[256]{0:T(256)S(1)} %bitcast.73), kind=kOutput, calls=%fused_computation.15.clone.1 | convolution fusion | flops 14156544 | bytes 1595392 | tf_op jit(solution)/shard_map/while/body/eval_jaxpr/dot_general | solution.py:62
  200.3 6.8 %fusion.66 = f32[1,3,1536]{2,1,0:T(4,128)S(1)} fusion(f32[3,1536]{1,0:T(4,128)S(1)} %fusion.65, f32[1536,256]{1,0:T(8,128)S(1)} %convolution_multiply_fusion.6, f32[1536]{0:T(1024)S(1)} %copy-done.1, f32[3,256]{1,0:T(4,128)S(1)} %get-tuple-element.355, f32[256]{0:T(256)S(1)} %bitcast.72), kind=kOutput, calls=%fused_computation.13.clone.1 | convolution fusion | flops 14165760 | bytes 1619968 | tf_op jit(solution)/shard_map/while/body/eval_jaxpr/dot_general | solution.py:62
  210.3 6.8 %fusion.65 = f32[3,1536]{1,0:T(4,128)S(1)} fusion(f32[1536,256]{1,0:T(8,128)S(1)} %convolution_multiply_fusion.6, f32[3,256]{1,0:T(4,128)S(1)} %get-tuple-element.355, f32[256]{0:T(256)S(1)} %bitcast.73), kind=kOutput, calls=%fused_computation.15.clone.1 | convolution fusion | flops 14156544 | bytes 1595392 | tf_op jit(solution)/shard_map/while/body/eval_jaxpr/dot_general | solution.py:62
  217.1 6.8 %fusion.66 = f32[1,3,1536]{2,1,0:T(4,128)S(1)} fusion(f32[3,1536]{1,0:T(4,128)S(1)} %fusion.65, f32[1536,256]{1,0:T(8,128)S(1)} %convolution_multiply_fusion.6, f32[1536]{0:T(1024)S(1)} %copy-done.1, f32[3,256]{1,0:T(4,128)S(1)} %get-tuple-element.355, f32[256]{0:T(256)S(1)} %bitcast.72), kind=kOutput, calls=%fused_computation.13.clone.1 | convolution fusion | flops 14165760 | bytes 1619968 | tf_op jit(solution)/shard_map/while/body/eval_jaxpr/dot_general | solution.py:62
  227.1 6.8 %fusion.65 = f32[3,1536]{1,0:T(4,128)S(1)} fusion(f32[1536,256]{1,0:T(8,128)S(1)} %convolution_multiply_fusion.6, f32[3,256]{1,0:T(4,128)S(1)} %get-tuple-element.355, f32[256]{0:T(256)S(1)} %bitcast.73), kind=kOutput, calls=%fused_computation.15.clone.1 | convolution fusion | flops 14156544 | bytes 1595392 | tf_op jit(solution)/shard_map/while/body/eval_jaxpr/dot_general | solution.py:62
  233.9 6.8 %fusion.66 = f32[1,3,1536]{2,1,0:T(4,128)S(1)} fusion(f32[3,1536]{1,0:T(4,128)S(1)} %fusion.65, f32[1536,256]{1,0:T(8,128)S(1)} %convolution_multiply_fusion.6, f32[1536]{0:T(1024)S(1)} %copy-done.1, f32[3,256]{1,0:T(4,128)S(1)} %get-tuple-element.355, f32[256]{0:T(256)S(1)} %bitcast.72), kind=kOutput, calls=%fused_computation.13.clone.1 | convolution fusion | flops 14165760 | bytes 1619968 | tf_op jit(solution)/shard_map/while/body/eval_jaxpr/dot_general | solution.py:62
  243.9 6.8 %fusion.65 = f32[3,1536]{1,0:T(4,128)S(1)} fusion(f32[1536,256]{1,0:T(8,128)S(1)} %convolution_multiply_fusion.6, f32[3,256]{1,0:T(4,128)S(1)} %get-tuple-element.355, f32[256]{0:T(256)S(1)} %bitcast.73), kind=kOutput, calls=%fused_computation.15.clone.1 | convolution fusion | flops 14156544 | bytes 1595392 | tf_op jit(solution)/shard_map/while/body/eval_jaxpr/dot_general | solution.py:62
  250.7 6.8 %fusion.66 = f32[1,3,1536]{2,1,0:T(4,128)S(1)} fusion(f32[3,1536]{1,0:T(4,128)S(1)} %fusion.65, f32[1536,256]{1,0:T(8,128)S(1)} %convolution_multiply_fusion.6, f32[1536]{0:T(1024)S(1)} %copy-done.1, f32[3,256]{1,0:T(4,128)S(1)} %get-tuple-element.355, f32[256]{0:T(256)S(1)} %bitcast.72), kind=kOutput, calls=%fused_computation.13.clone.1 | convolution fusion | flops 14165760 | bytes 1619968 | tf_op jit(solution)/shard_map/while/body/eval_jaxpr/dot_general | solution.py:62
  260.7 6.8 %fusion.65 = f32[3,1536]{1,0:T(4,128)S(1)} fusion(f32[1536,256]{1,0:T(8,128)S(1)} %convolution_multiply_fusion.6, f32[3,256]{1,0:T(4,128)S(1)} %get-tuple-element.355, f32[256]{0:T(256)S(1)} %bitcast.73), kind=kOutput, calls=%fused_computation.15.clone.1 | convolution fusion | flops 14156544 | bytes 1595392 | tf_op jit(solution)/shard_map/while/body/eval_jaxpr/dot_general | solution.py:62
  267.5 6.8 %fusion.66 = f32[1,3,1536]{2,1,0:T(4,128)S(1)} fusion(f32[3,1536]{1,0:T(4,128)S(1)} %fusion.65, f32[1536,256]{1,0:T(8,128)S(1)} %convolution_multiply_fusion.6, f32[1536]{0:T(1024)S(1)} %copy-done.1, f32[3,256]{1,0:T(4,128)S(1)} %get-tuple-element.355, f32[256]{0:T(256)S(1)} %bitcast.72), kind=kOutput, calls=%fused_computation.13.clone.1 | convolution fusion | flops 14165760 | bytes 1619968 | tf_op jit(solution)/shard_map/while/body/eval_jaxpr/dot_general | solution.py:62
  277.5 6.8 %fusion.65 = f32[3,1536]{1,0:T(4,128)S(1)} fusion(f32[1536,256]{1,0:T(8,128)S(1)} %convolution_multiply_fusion.6, f32[3,256]{1,0:T(4,128)S(1)} %get-tuple-element.355, f32[256]{0:T(256)S(1)} %bitcast.73), kind=kOutput, calls=%fused_computation.15.clone.1 | convolution fusion | flops 14156544 | bytes 1595392 | tf_op jit(solution)/shard_map/while/body/eval_jaxpr/dot_general | solution.py:62
  284.2 6.8 %fusion.66 = f32[1,3,1536]{2,1,0:T(4,128)S(1)} fusion(f32[3,1536]{1,0:T(4,128)S(1)} %fusion.65, f32[1536,256]{1,0:T(8,128)S(1)} %convolution_multiply_fusion.6, f32[1536]{0:T(1024)S(1)} %copy-done.1, f32[3,256]{1,0:T(4,128)S(1)} %get-tuple-element.355, f32[256]{0:T(256)S(1)} %bitcast.72), kind=kOutput, calls=%fused_computation.13.clone.1 | convolution fusion | flops 14165760 | bytes 1619968 | tf_op jit(solution)/shard_map/while/body/eval_jaxpr/dot_general | solution.py:62
  294.2 6.8 %fusion.65 = f32[3,1536]{1,0:T(4,128)S(1)} fusion(f32[1536,256]{1,0:T(8,128)S(1)} %convolution_multiply_fusion.6, f32[3,256]{1,0:T(4,128)S(1)} %get-tuple-element.355, f32[256]{0:T(256)S(1)} %bitcast.73), kind=kOutput, calls=%fused_computation.15.clone.1 | convolution fusion | flops 14156544 | bytes 1595392 | tf_op jit(solution)/shard_map/while/body/eval_jaxpr/dot_general | solution.py:62
  301.0 6.8 %fusion.66 = f32[1,3,1536]{2,1,0:T(4,128)S(1)} fusion(f32[3,1536]{1,0:T(4,128)S(1)} %fusion.65, f32[1536,256]{1,0:T(8,128)S(1)} %convolution_multiply_fusion.6, f32[1536]{0:T(1024)S(1)} %copy-done.1, f32[3,256]{1,0:T(4,128)S(1)} %get-tuple-element.355, f32[256]{0:T(256)S(1)} %bitcast.72), kind=kOutput, calls=%fused_computation.13.clone.1 | convolution fusion | flops 14165760 | bytes 1619968 | tf_op jit(solution)/shard_map/while/body/eval_jaxpr/dot_general | solution.py:62
  309.6 49.3 %all-reduce.3.cloned.1.call-done = f32[8,3,1536]{2,0,1:T(8,128)} async-done(((f32[8,3,1536]{2,0,1:T(8,128)}), f32[8,3,1536]{2,0,1:T(8,128)}) %all-reduce.3.cloned.1.call-update) | async-done | bytes 147472 | tf_op jit(solution)/shard_map/psum | solution.py:98
  (134 shorter events, 140.2 us)
Async XLA Ops:
  9.1 8.2 %copy-start.3 = (s32[3,256]{1,0:T(4,128)S(1)}, s32[3,256]{1,0:T(4,128)}, u32[]{:S(2)}) copy-start(s32[3,256]{1,0:T(4,128)} %param.9) | copy-start | bytes 9220
  9.1 8.9 %copy-start.4 = (s32[1536]{0:T(1024)S(1)}, s32[1536]{0:T(1024)}, u32[]{:S(2)}) copy-start(s32[1536]{0:T(1024)} %param.10) | copy-start | bytes 18436
  9.2 8.9 %copy-start.7 = (f32[4]{0:T(128)S(1)}, f32[4]{0:T(128)}, u32[]{:S(2)}) copy-start(f32[4]{0:T(128)} %param.11) | copy-start | bytes 52
  11.7 12.5 %all-to-all-start = ((f32[8,1,9216]{2,1,0:T(1,128)}), f32[8,1,9216]{2,1,0:T(1,128)S(1)}, u32[]{:S(2)}, u32[]{:S(2)}) async-start(f32[8,1,9216]{2,1,0:T(1,128)} %reshape.163), calls=%async_computation | async-start | bytes 589824 | tf_op jit(solution)/shard_map/all_to_all | solution.py:85
  16.9 341.9 %all-reduce.3.cloned.1.call-start = ((), (), s32[]{:S(2)}) async-start(), calls=%async_computation.1 | async-start | bytes 294912 | tf_op jit(solution)/shard_map/psum | solution.py:98
  18.1 6.1 %copy-start = (f32[1536]{0:T(1024)}, f32[1536]{0:T(1024)S(1)}, u32[]{:S(2)}) copy-start(f32[1536]{0:T(1024)S(1)} %select_reduce_fusion) | copy-start | bytes 18436
  49.1 1.2 copy-start.5
  49.1 1.2 copy-start.6
  50.3 125.0 %copy-start.2 = (f32[256]{0:T(256)S(1)}, f32[256]{0:T(256)}, u32[]{:S(2)}) copy-start(f32[256]{0:T(256)} %multiply_divide_fusion) | copy-start | bytes 3076
  175.3 8.3 %copy-start.1 = (f32[1536]{0:T(1024)S(1)}, f32[1536]{0:T(1024)}, u32[]{:S(2)}) copy-start(f32[1536]{0:T(1024)} %get-tuple-element.352) | copy-start | bytes 18436 | tf_op jit(solution)/shard_map/while
  192.1 8.3 %copy-start.1 = (f32[1536]{0:T(1024)S(1)}, f32[1536]{0:T(1024)}, u32[]{:S(2)}) copy-start(f32[1536]{0:T(1024)} %get-tuple-element.352) | copy-start | bytes 18436 | tf_op jit(solution)/shard_map/while
  208.9 8.3 %copy-start.1 = (f32[1536]{0:T(1024)S(1)}, f32[1536]{0:T(1024)}, u32[]{:S(2)}) copy-start(f32[1536]{0:T(1024)} %get-tuple-element.352) | copy-start | bytes 18436 | tf_op jit(solution)/shard_map/while
  225.6 8.3 %copy-start.1 = (f32[1536]{0:T(1024)S(1)}, f32[1536]{0:T(1024)}, u32[]{:S(2)}) copy-start(f32[1536]{0:T(1024)} %get-tuple-element.352) | copy-start | bytes 18436 | tf_op jit(solution)/shard_map/while
  242.4 8.3 %copy-start.1 = (f32[1536]{0:T(1024)S(1)}, f32[1536]{0:T(1024)}, u32[]{:S(2)}) copy-start(f32[1536]{0:T(1024)} %get-tuple-element.352) | copy-start | bytes 18436 | tf_op jit(solution)/shard_map/while
  259.2 8.3 %copy-start.1 = (f32[1536]{0:T(1024)S(1)}, f32[1536]{0:T(1024)}, u32[]{:S(2)}) copy-start(f32[1536]{0:T(1024)} %get-tuple-element.352) | copy-start | bytes 18436 | tf_op jit(solution)/shard_map/while
  276.0 8.3 %copy-start.1 = (f32[1536]{0:T(1024)S(1)}, f32[1536]{0:T(1024)}, u32[]{:S(2)}) copy-start(f32[1536]{0:T(1024)} %get-tuple-element.352) | copy-start | bytes 18436 | tf_op jit(solution)/shard_map/while
  292.7 8.3 %copy-start.1 = (f32[1536]{0:T(1024)S(1)}, f32[1536]{0:T(1024)}, u32[]{:S(2)}) copy-start(f32[1536]{0:T(1024)} %get-tuple-element.352) | copy-start | bytes 18436 | tf_op jit(solution)/shard_map/while
Sparse Core Ops, SparseCore 0:
  309.7 49.1 all-reduce.2
where the time goes:
time: 368 us
  matrix products  228 us (62%)
  waiting for transfers between devices  55 us (15%)
  blocking collectives  37.6 us (10%)
  local copies, waits for them, and re-layouts  25.1 us (7%)
  between operations  13.6 us (4%)
  starting transfers between devices  5.21 us (1%)
    dot_general x8, matrix products, forces(): jnp.dot(right, jnp.cos(angle), precision=lax.Precision.HIGHEST)  54.3 us
    dot_general x8, matrix products, forces(): jnp.dot(left, jnp.sin(angle), precision=lax.Precision.HIGHEST)  54.3 us
    psum x1, waiting for transfers between devices, local(): summed = lax.psum(partial_force, 'bead')  49.3 us
    dot_general x8, matrix products, structure(): jnp.dot(jnp.sin(angle), charge, precision=lax.Precision.HIGHEST)  46.8 us
    dot_general x8, matrix products, structure(): jnp.dot(jnp.cos(angle), charge, precision=lax.Precision.HIGHEST)  46.4 us
    dot_general x16, matrix products, phases(): jnp.dot(fourier_mode_table.T, position, precision=lax.Precision.HIGHEST)  23.3 us
    psum x1, blocking collectives, local(): cos_fac, sin_fac = lax.psum((cos_part, sin_part), 'atom')  19 us
    all_gather x1, blocking collectives, local(): contracted = lax.all_gather(portion, 'bead', axis=2, tiled=True)  18.6 us
  transfers between devices with their start and end apart: 2, of which 2 were waited for; matrix products, arithmetic and copies ran while one was open for 0% of the time, Pallas kernels for 0%

commit v1 on v0

v1 whole, which is shorter than its diff:
```python
import functools
import math

import jax
import jax.numpy as jnp
import numpy as np
from jax import lax
from jax.experimental import pallas as pl
from jax.experimental.pallas import tpu as pltpu
from jax.sharding import PartitionSpec as P

CONTR = 8
REACH = 10
ROWS = 24
HALF = 16
GRID = HALF + REACH * ROWS
TWO_PI = 2.0 * math.pi
MESH = pl.DeviceIdType.MESH
LANES = 128


def _sine_coefficients():
    u = np.cos(np.pi * (np.arange(400) + 0.5) / 400)
    square = 0.125 + 0.125 * u
    r = np.sqrt(square)
    value = np.sin(2 * np.pi * r) / (r * (0.25 - square))
    return [float(c) for c in np.polynomial.polynomial.polyfit(square, value, 5)]


SINE = _sine_coefficients()


def sin_turns(turns):
    r = turns - jnp.round(turns)
    square = r * r
    p = SINE[5]
    for c in SINE[4::-1]:
        p = p * square + c
    return r * (0.25 - square) * p


def cos_turns(turns):
    return sin_turns(turns + 0.25)


def split(value):
    high = value.astype(jnp.bfloat16)
    low = (value - high.astype(jnp.float32)).astype(jnp.bfloat16)
    return high, low


def cycle_table(j, b, beads):
    shift = j / CONTR - b / beads
    total = jnp.ones_like(shift)
    for c in range(1, CONTR // 2):
        total = total + 2.0 * cos_turns(c * shift)
    last = cos_turns(0.5 * j) * cos_turns((CONTR // 2) * b / beads)
    total = total + math.sqrt(2.0) * last
    return total / beads


def dot_nn(a, b):
    return lax.dot_general(a, b, (((1,), (0,)), ((), ())), preferred_element_type=jnp.float32)


def dot_nt(a, b):
    return lax.dot_general(a, b, (((1,), (1,)), ((), ())), preferred_element_type=jnp.float32)


def kernel(
    nb, na, values_ref, pos_ref, wave_ref, label_ref, out_ref,
    part, land, site, waves, charge, xy_high, xy_low, z_mat, z_wave, factor, factor_land, force,
    send_wave, recv_wave, send_part, recv_part, send_fac, recv_fac, send_force, recv_force,
):
    share = nb // CONTR
    local_beads, sites = pos_ref.shape[1], pos_ref.shape[2]
    beads = local_beads * nb
    own_sites = sites // share
    tiles = own_sites // LANES
    rows = part.shape[1]
    kvec = wave_ref.shape[1]
    group = na * share
    me = lax.axis_index("bead")
    atom = lax.axis_index("atom")
    bead, chunk = me // share, lax.rem(me, share)

    def bead_peer(d):
        return (lax.rem(me + d, nb), atom)

    def group_peer(d):
        other = bead * share + lax.rem(chunk + d % share, share)
        return (other, lax.rem(atom + d // share, na))

    barrier = pltpu.get_barrier_semaphore()
    peers = [bead_peer(d) for d in range(1, nb)]
    peers += [group_peer(d) for d in range(1, group) if d >= share]
    for peer in peers:
        pl.semaphore_signal(barrier, inc=1, device_id=peer, device_id_type=MESH)

    waves[me] = jnp.zeros((8, kvec), jnp.float32)
    waves[me, 0:3, :] = wave_ref[...].astype(jnp.float32)

    lane = lax.broadcasted_iota(jnp.int32, (8, LANES), 1)
    sub = lax.broadcasted_iota(jnp.int32, (8, LANES), 0)
    first = me * local_beads
    table = cycle_table(sub.astype(jnp.float32), (first + lane).astype(jnp.float32), beads)
    columns = [jnp.broadcast_to(table[:, b : b + 1], (8, LANES)) for b in range(local_beads)]
    for x in range(3):
        for t in range(sites // LANES):
            total = None
            for b in range(local_beads):
                term = columns[b] * pos_ref[x, b : b + 1, t * LANES : (t + 1) * LANES]
                total = term if total is None else total + term
            c, row = t // tiles, x * tiles + t % tiles
            for j in range(CONTR):
                part[j * share + c, row : row + 1, :] = total[j : j + 1, :]

    pl.semaphore_wait(barrier, len(peers))

    part_copies, wave_copies = [], []
    for d in range(1, nb):
        peer = bead_peer(d)
        copy = pltpu.make_async_remote_copy(
            src_ref=part.at[peer[0]], dst_ref=land.at[d], send_sem=send_part.at[d],
            recv_sem=recv_part.at[d], device_id=peer, device_id_type=MESH,
        )
        copy.start()
        part_copies.append(copy)
    for d in range(1, nb):
        copy = pltpu.make_async_remote_copy(
            src_ref=waves.at[me], dst_ref=waves.at[me], send_sem=send_wave.at[d],
            recv_sem=recv_wave.at[d], device_id=bead_peer(d), device_id_type=MESH,
        )
        copy.start()
        wave_copies.append(copy)

    label = label_ref[...]
    q = jnp.zeros(label.shape, jnp.float32)
    for kind in range(values_ref.shape[0]):
        q = q + jnp.where(label == kind, values_ref[kind], 0.0)
    for c in range(share):
        charge[c, 0:tiles, :] = q[c * tiles : (c + 1) * tiles, :]

    for copy in part_copies:
        copy.wait()
    total = part[me]
    for d in range(1, nb):
        total = total + land[d]
    site[...] = total

    row_id = lax.broadcasted_iota(jnp.int32, (ROWS, LANES), 0)
    second = jnp.where(row_id < ROWS - REACH, row_id, row_id - ROWS).astype(jnp.float32)
    third = (row_id - REACH).astype(jnp.float32)

    def reduced(row):
        x = site[pl.ds(row, 1), :]
        return x - jnp.round(x)

    def build(t, carry):
        where = pl.ds(pl.multiple_of(t * LANES, LANES), LANES)
        x = jnp.broadcast_to(reduced(t), (ROWS, LANES))
        y = second * reduced(tiles + t)
        z = third * reduced(2 * tiles + t)
        step_r, step_i = cos_turns(x), sin_turns(x)
        real, imag = cos_turns(y), sin_turns(y)
        reals, imags = [real[:HALF]], [imag[:HALF]]
        for a in range(REACH):
            real, imag = real * step_r - imag * step_i, real * step_i + imag * step_r
            reals.append(real)
            imags.append(imag)
        for base, parts in ((0, reals), (GRID, imags)):
            blocks = [parts[0]]
            for a in range(1, REACH + 1, 2):
                blocks.append(jnp.concatenate(parts[a : a + 2], axis=0))
            at = base
            for block in blocks:
                high, low = split(block)
                xy_high[at : at + block.shape[0], where] = high
                xy_low[at : at + block.shape[0], where] = low
                at += block.shape[0]
        cos_z, sin_z = cos_turns(z), sin_turns(z)
        z_wave[0, :, where] = cos_z
        z_wave[1, :, where] = sin_z
        q_row = charge[chunk, pl.ds(t, 1), :]
        qc, qs = q_row * cos_z, q_row * sin_z
        for n, block in enumerate(((qc, qs), (-qs, qc))):
            high, low = split(jnp.concatenate(block, axis=0))
            z_mat[n, 0 : 2 * ROWS, where] = high
            z_mat[n, 2 * ROWS : 4 * ROWS, where] = low
        return carry

    lax.fori_loop(0, tiles, build, 0)

    product = dot_nt(z_mat[0], xy_high[0:GRID, :]) + dot_nt(z_mat[1], xy_high[GRID : 2 * GRID, :])
    own = product[: 2 * ROWS] + product[2 * ROWS :]
    own = own + dot_nt(z_mat[0, 0 : 2 * ROWS, :], xy_low[0:GRID, :])
    own = own + dot_nt(z_mat[1, 0 : 2 * ROWS, :], xy_low[GRID : 2 * GRID, :])
    factor[...] = own

    factor_copies = []
    for d in range(1, group):
        copy = pltpu.make_async_remote_copy(
            src_ref=factor, dst_ref=factor_land.at[d], send_sem=send_fac.at[d],
            recv_sem=recv_fac.at[d], device_id=group_peer(d), device_id_type=MESH,
        )
        copy.start()
        factor_copies.append(copy)

    for copy in wave_copies:
        copy.wait()
    count = jnp.zeros((ROWS, GRID), jnp.float32)
    pair_id = lax.broadcasted_iota(jnp.int32, (GRID, kvec), 0).astype(jnp.float32)
    third_id = lax.broadcasted_iota(jnp.int32, (ROWS, kvec), 0).astype(jnp.float32)
    for n in range(nb):
        m = waves[n]
        m0, m1, m2 = m[0:1], m[1:2], m[2:3]
        wrapped = jnp.where(m1 < 0.0, m1 + ROWS, m1)
        pair = jnp.where(m0 > 0.0, HALF + (m0 - 1.0) * ROWS + wrapped, m1)
        hot_pair = jnp.where(pair_id == pair, 1.0, 0.0).astype(jnp.bfloat16)
        hot_third = jnp.where(third_id == m2 + REACH, 1.0, 0.0).astype(jnp.bfloat16)
        count = count + dot_nt(hot_third, hot_pair)
    col = lax.broadcasted_iota(jnp.int32, (ROWS, GRID), 1)
    line = lax.broadcasted_iota(jnp.int32, (ROWS, GRID), 0)
    f0 = jnp.zeros((ROWS, GRID), jnp.int32)
    for a in range(REACH):
        f0 = f0 + jnp.where(col >= HALF + a * ROWS, 1, 0)
    f1 = jnp.where(f0 > 0, col - HALF - (f0 - 1) * ROWS, col)
    f1 = jnp.where(f1 < ROWS - REACH, f1, f1 - ROWS)
    f2 = line - REACH
    f0, f1, f2 = f0.astype(jnp.float32), f1.astype(jnp.float32), f2.astype(jnp.float32)
    msq = f0 * f0 + f1 * f1 + f2 * f2
    weight = 4.0 * jnp.exp(-msq / 100.0) / (jnp.maximum(msq, 1.0) * float(sites * na))
    weight = weight * count

    for copy in factor_copies:
        copy.wait()
    total = factor[...]
    for d in range(1, group):
        total = total + factor_land[d]
    gr, gi = weight * total[:ROWS], weight * total[ROWS:]
    u, v = jnp.concatenate([-gi, gr], axis=1), jnp.concatenate([gr, gi], axis=1)
    w0, w1 = jnp.concatenate([f0, f0], axis=1), jnp.concatenate([f1, f1], axis=1)
    left = jnp.concatenate([u, v, w0 * u, w0 * v, w1 * u, w1 * v], axis=0)
    left_high, left_low = split(left)
    left_both = jnp.concatenate([left_high, left_low], axis=0)
    height = 6 * ROWS

    width = 2 * LANES if tiles % 2 == 0 else LANES
    per = width // LANES
    m2_rows = (lax.broadcasted_iota(jnp.int32, (ROWS, width), 0) - REACH).astype(jnp.float32)
    for n in range(own_sites // width):
        where = slice(n * width, (n + 1) * width)
        both = dot_nn(left_both, xy_high[:, where])
        term = both[:height] + both[height:] + dot_nn(left_high, xy_low[:, where])
        cz, sz = z_wave[0, :, where], z_wave[1, :, where]
        pieces = [
            term[2 * i * ROWS : (2 * i + 1) * ROWS] * cz
            + term[(2 * i + 1) * ROWS : (2 * i + 2) * ROWS] * sz
            for i in range(3)
        ]
        along = (pieces[1], pieces[2], pieces[0] * m2_rows)
        for x in range(3):
            summed = TWO_PI * jnp.sum(along[x], axis=0, keepdims=True)
            for p in range(per):
                t = n * per + p
                q_row = charge[chunk, t : t + 1, :]
                force[me, x * tiles + t : x * tiles + t + 1, :] = (
                    q_row * summed[:, p * LANES : (p + 1) * LANES]
                )

    force_copies = []
    for d in range(1, nb):
        copy = pltpu.make_async_remote_copy(
            src_ref=force.at[me], dst_ref=force.at[me], send_sem=send_force.at[d],
            recv_sem=recv_force.at[d], device_id=bead_peer(d), device_id_type=MESH,
        )
        copy.start()
        force_copies.append(copy)
    sub_b = lax.broadcasted_iota(jnp.int32, (local_beads, LANES), 0)
    lane_j = lax.broadcasted_iota(jnp.int32, (local_beads, LANES), 1)
    turned = cycle_table(lane_j.astype(jnp.float32), (first + sub_b).astype(jnp.float32), beads)
    spread = [jnp.broadcast_to(turned[:, j : j + 1], (local_beads, LANES)) for j in range(CONTR)]
    for copy in force_copies:
        copy.wait()
    for x in range(3):
        for t in range(sites // LANES):
            c, row = t // tiles, x * tiles + t % tiles
            total = None
            for j in range(CONTR):
                term = spread[j] * force[j * share + c, row : row + 1, :]
                total = term if total is None else total + term
            out_ref[x, :, t * LANES : (t + 1) * LANES] = total


def local(nb, na, positions, waves, labels, values):
    local_beads, _, sites = positions.shape
    kvec = waves.shape[1]
    share = nb // CONTR
    own_sites = sites // share
    tiles = own_sites // LANES
    rows = -(-3 * tiles // 8) * 8
    group = na * share
    dma = pltpu.SemaphoreType.DMA
    vmem = pl.BlockSpec(memory_space=pltpu.VMEM)
    out = pl.pallas_call(
        functools.partial(kernel, nb, na),
        out_shape=jax.ShapeDtypeStruct((3, local_beads, sites), jnp.float32),
        in_specs=[pl.BlockSpec(memory_space=pltpu.SMEM), vmem, vmem, vmem],
        out_specs=vmem,
        scratch_shapes=[
            pltpu.VMEM((nb, rows, LANES), jnp.float32),
            pltpu.VMEM((nb, rows, LANES), jnp.float32),
            pltpu.VMEM((rows, LANES), jnp.float32),
            pltpu.VMEM((nb, 8, kvec), jnp.float32),
            pltpu.VMEM((share, -(-tiles // 8) * 8, LANES), jnp.float32),
            pltpu.VMEM((2 * GRID, own_sites), jnp.bfloat16),
            pltpu.VMEM((2 * GRID, own_sites), jnp.bfloat16),
            pltpu.VMEM((2, 4 * ROWS, own_sites), jnp.bfloat16),
            pltpu.VMEM((2, ROWS, own_sites), jnp.float32),
            pltpu.VMEM((2 * ROWS, GRID), jnp.float32),
            pltpu.VMEM((group, 2 * ROWS, GRID), jnp.float32),
            pltpu.VMEM((nb, rows, LANES), jnp.float32),
            dma((nb,)), dma((nb,)), dma((nb,)), dma((nb,)),
            dma((group,)), dma((group,)), dma((nb,)), dma((nb,)),
        ],
        compiler_params=pltpu.CompilerParams(
            collective_id=0, has_side_effects=True, vmem_limit_bytes=40 * 1024 * 1024
        ),
    )(values, jnp.transpose(positions, (1, 0, 2)), waves, labels.reshape(-1, LANES))
    return jnp.transpose(out, (1, 0, 2))


def solution(mesh):
    in_specs = (P("bead", None, "atom"), P(None, "bead"), P("atom"), P())
    out_specs = P("bead", None, "atom")
    body = functools.partial(local, mesh.shape["bead"], mesh.shape["atom"])
    return jax.shard_map(body, mesh=mesh, in_specs=in_specs, out_specs=out_specs, check_vma=False)
```

time: 368 us -> 28.3 us (0.08)
  matrix products: 228 us -> 0 us
  waiting for transfers between devices: 55 us -> 0 us
  blocking collectives: 37.6 us -> 0 us
  Pallas kernels: 0 us -> 24.4 us
  local copies, waits for them, and re-layouts: 25.1 us -> 3.71 us
  between operations: 13.6 us -> 0.01 us
  starting transfers between devices: 5.21 us -> 0 us
    dot_general x51 -> x0, matrix products: 228 us -> none  [the longest x8 54.3 us: forces(): jnp.dot(right, jnp.cos(angle), precision=lax.Precision.HIGHEST)]
    psum x1 -> x0, waiting for transfers between devices: 49.3 us -> none  [local(): summed = lax.psum(partial_force, 'bead')]
    pallas_call x0 -> x1, Pallas kernels: none -> 24.4 us  [local(): pl.pallas_call(functools.partial(kernel, nb, na), out_shape=jax.ShapeDtyp...]
    psum x1 -> x0, blocking collectives: 19 us -> none  [local(): cos_fac, sin_fac = lax.psum((cos_part, sin_part), 'atom')]
    all_gather x1 -> x0, blocking collectives: 18.6 us -> none  [local(): contracted = lax.all_gather(portion, 'bead', axis=2, tiled=True)]
    dynamic_update_slice x32 -> x0, local copies, waits for them, and re-layouts: 14 us -> none  [the longest x16 13.6 us: force_parts(): return lax.map(forces, (contracted, cos_fac, sin_fac))]
    all_to_all x1 -> x0, waiting for transfers between devices: 5.72 us -> none  [local(): lax.all_to_all(replica_point_fractions, 'bead', split_axis=2, concat_axis...]
    all_to_all x1 -> x0, starting transfers between devices: 5.17 us -> none  [local(): lax.all_to_all(replica_point_fractions, 'bead', split_axis=2, concat_axis...]
  transfers between devices with their start and end apart: 2 -> 0, of which waited for: 2 -> 0; matrix products, arithmetic and copies ran while one was open for 0% -> 0% of each run, Pallas kernels for 0% -> 0%
where the time goes in v1:
time: 28.3 us; the launch traced here: 28.1 us
  Pallas kernels  24.4 us (86%)
  local copies, waits for them, and re-layouts  3.71 us (13%)
    pallas_call x1, Pallas kernels, local(): pl.pallas_call(functools.partial(kernel, nb, na), out_shape=jax.ShapeDtyp...  24.4 us
    unnamed x9, local copies, waits for them, and re-layouts  3.71 us

profile of v1, /device:TPU:0, one launch (start us, length us, event | category | flops | bytes accessed | tf_op | source)
XLA Modules:
  0.0 28.1 jit_solution(1345750452741017777)
XLA Ops:
  0.0 0.0 copy-start.3
  0.0 0.7 %copy-done.3 = f32[4]{0:T(128)S(1)} copy-done((f32[4]{0:T(128)S(1)}, f32[4]{0:T(128)}, u32[]{:S(2)}) %copy-start.3) | copy-done | bytes 40
  0.7 0.0 copy-start
  0.7 1.0 %copy-done = f32[16,3,1536]{2,0,1:T(8,128)S(1)} copy-done((f32[16,3,1536]{2,0,1:T(8,128)S(1)}, f32[16,3,1536]{2,0,1:T(8,128)}, u32[]{:S(2)}) %copy-start) | copy-done | bytes 294936
  1.6 0.0 copy-start.1
  1.6 0.7 %copy-done.1 = s32[1536]{0:T(1024)S(1)} copy-done((s32[1536]{0:T(1024)S(1)}, s32[1536]{0:T(1024)}, u32[]{:S(2)}) %copy-start.1) | copy-done | bytes 6168
  2.3 0.0 copy-start.2
  2.3 0.7 %copy-done.2 = s32[3,256]{1,0:T(4,128)S(1)} copy-done((s32[3,256]{1,0:T(4,128)S(1)}, s32[3,256]{1,0:T(4,128)}, u32[]{:S(2)}) %copy-start.2) | copy-done | bytes 3096
  3.0 24.4 %shard_map.46 = f32[3,16,1536]{2,1,0:T(8,128)S(1)} custom-call(f32[4]{0:T(128)S(1)} %copy-done.3, f32[3,16,1536]{2,1,0:T(8,128)S(1)} %bitcast.4, s32[3,256]{1,0:T(4,128)S(1)} %copy-done.2, s32[12,128]{1,0:T(8,128)S(1)} %bitcast.5), custom_call_target="tpu_custom_call" | custom-call | tf_op jit(solution)/shard_map/pallas_call | solution.py:305
  27.4 0.7 %copy.6 = f32[16,3,1536]{2,0,1:T(8,128)} copy(f32[16,3,1536]{2,0,1:T(8,128)S(1)} %bitcast.3) | data formatting | bytes 589824
Async XLA Ops:
  0.0 0.7 %copy-start.3 = (f32[4]{0:T(128)S(1)}, f32[4]{0:T(128)}, u32[]{:S(2)}) copy-start(f32[4]{0:T(128)} %values_ref.1) | copy-start | bytes 52
  0.7 1.0 %copy-start = (f32[16,3,1536]{2,0,1:T(8,128)S(1)}, f32[16,3,1536]{2,0,1:T(8,128)}, u32[]{:S(2)}) copy-start(f32[16,3,1536]{2,0,1:T(8,128)} %param.4) | copy-start | bytes 884740
  1.6 0.7 %copy-start.1 = (s32[1536]{0:T(1024)S(1)}, s32[1536]{0:T(1024)}, u32[]{:S(2)}) copy-start(s32[1536]{0:T(1024)} %param.6) | copy-start | bytes 18436
  2.3 0.7 %copy-start.2 = (s32[3,256]{1,0:T(4,128)S(1)}, s32[3,256]{1,0:T(4,128)}, u32[]{:S(2)}) copy-start(s32[3,256]{1,0:T(4,128)} %wave_ref.1) | copy-start | bytes 9220

commit v2 on v1

v2 whole, which is shorter than its diff:
```python
import functools
import math

import jax
import jax.numpy as jnp
import numpy as np
from jax import lax
from jax.experimental import pallas as pl
from jax.experimental.pallas import tpu as pltpu
from jax.sharding import PartitionSpec as P

CONTR = 8
REACH = 10
ROWS = 24
HALF = 16
GRID = HALF + REACH * ROWS
TWO_PI = 2.0 * math.pi
MESH = pl.DeviceIdType.MESH
LANES = 128


def _sine_coefficients():
    u = np.cos(np.pi * (np.arange(400) + 0.5) / 400)
    square = 0.125 + 0.125 * u
    r = np.sqrt(square)
    value = np.sin(2 * np.pi * r) / (r * (0.25 - square))
    return [float(c) for c in np.polynomial.polynomial.polyfit(square, value, 5)]


SINE = _sine_coefficients()


def sin_turns(turns):
    r = turns - jnp.round(turns)
    square = r * r
    p = SINE[5]
    for c in SINE[4::-1]:
        p = p * square + c
    return r * (0.25 - square) * p


def cos_turns(turns):
    return sin_turns(turns + 0.25)


def split(value):
    high = value.astype(jnp.bfloat16)
    low = (value - high.astype(jnp.float32)).astype(jnp.bfloat16)
    return high, low


def cycle_table(j, b, beads):
    shift = j / CONTR - b / beads
    total = jnp.ones_like(shift)
    for c in range(1, CONTR // 2):
        total = total + 2.0 * cos_turns(c * shift)
    last = cos_turns(0.5 * j) * cos_turns((CONTR // 2) * b / beads)
    total = total + math.sqrt(2.0) * last
    return total / beads


def dot_nn(a, b):
    return lax.dot_general(a, b, (((1,), (0,)), ((), ())), preferred_element_type=jnp.float32)


def dot_nt(a, b):
    return lax.dot_general(a, b, (((1,), (1,)), ((), ())), preferred_element_type=jnp.float32)


def kernel(
    nb, na, values_hbm, pos_hbm, wave_hbm, label_hbm, out_hbm,
    out_ref, values, pos, wave_in, label_in,
    part, land, site, waves, charge, xy_high, xy_low, z_mat, z_wave, factor, factor_land, whole, turned, force,
    in_sem, pos_sem, out_sem, send_wave, recv_wave, send_part, recv_part, send_fac, recv_fac, send_all, recv_all,
    send_force, recv_force,
):
    share = nb // CONTR
    local_beads, sites = pos.shape[1], pos.shape[2]
    beads = local_beads * nb
    own_sites = sites // share
    tiles = own_sites // LANES
    chunks = site.shape[0]
    span = tiles // chunks
    kvec = wave_in.shape[1]
    group = na * share
    me = lax.axis_index("bead")
    atom = lax.axis_index("atom")
    bead, chunk = me // share, lax.rem(me, share)
    place = atom * share + chunk

    def bead_peer(d):
        return (lax.rem(me + d, nb), atom)

    def group_peer(d):
        other = bead * share + lax.rem(chunk + d % share, share)
        return (other, lax.rem(atom + d // share, na))

    barrier = pltpu.get_barrier_semaphore()
    peers = [bead_peer(d) for d in range(1, nb)]
    peers += [group_peer(d) for d in range(1, group) if d >= share]
    for peer in peers:
        pl.semaphore_signal(barrier, inc=1, device_id=peer, device_id_type=MESH)

    wave_copy = pltpu.make_async_copy(wave_hbm, wave_in, in_sem.at[0])
    wave_copy.start()
    pos_copies = []
    for n in range(chunks):
        for c in range(share):
            where = pl.ds((c * tiles + n * span) * LANES, span * LANES)
            copy = pltpu.make_async_copy(
                pos_hbm.at[:, :, where], pos.at[:, :, where], pos_sem.at[n * share + c]
            )
            copy.start()
            pos_copies.append(copy)
    label_copy = pltpu.make_async_copy(label_hbm, label_in, in_sem.at[1])
    label_copy.start()
    value_copy = pltpu.make_async_copy(values_hbm, values, in_sem.at[2])
    value_copy.start()

    lane = lax.broadcasted_iota(jnp.int32, (8, LANES), 1)
    sub = lax.broadcasted_iota(jnp.int32, (8, LANES), 0)
    first = me * local_beads
    table = cycle_table(sub.astype(jnp.float32), (first + lane).astype(jnp.float32), beads)
    columns = [jnp.broadcast_to(table[:, b : b + 1], (8, LANES)) for b in range(local_beads)]

    wave_copy.wait()
    waves[me] = jnp.zeros((8, kvec), jnp.float32)
    waves[me, 0:3, :] = wave_in[...].astype(jnp.float32)

    part_copies, wave_copies = [], []
    for n in range(chunks):
        for c in range(share):
            pos_copies[n * share + c].wait()
            for x in range(3):
                for t in range(span):
                    at = (c * tiles + n * span + t) * LANES
                    total = None
                    for b in range(local_beads):
                        term = columns[b] * pos[x, b : b + 1, at : at + LANES]
                        total = term if total is None else total + term
                    row = x * span + t
                    for j in range(CONTR):
                        part[j * share + c, n, row : row + 1, :] = total[j : j + 1, :]
        if n == 0:
            pl.semaphore_wait(barrier, len(peers))
        for d in range(1, nb):
            peer = bead_peer(d)
            copy = pltpu.make_async_remote_copy(
                src_ref=part.at[peer[0], n], dst_ref=land.at[d, n], send_sem=send_part.at[n, d],
                recv_sem=recv_part.at[n, d], device_id=peer, device_id_type=MESH,
            )
            copy.start()
            part_copies.append(copy)
    for d in range(1, nb):
        copy = pltpu.make_async_remote_copy(
            src_ref=waves.at[me], dst_ref=waves.at[me], send_sem=send_wave.at[d],
            recv_sem=recv_wave.at[d], device_id=bead_peer(d), device_id_type=MESH,
        )
        copy.start()
        wave_copies.append(copy)

    label_copy.wait()
    value_copy.wait()
    label = label_in[...]
    q = jnp.zeros(label.shape, jnp.float32)
    for kind in range(values.shape[0]):
        q = q + jnp.where(label == kind, values[kind], 0.0)
    for c in range(share):
        charge[c, 0:tiles, :] = q[c * tiles : (c + 1) * tiles, :]
    sub_b = lax.broadcasted_iota(jnp.int32, (local_beads, LANES), 0)
    lane_j = lax.broadcasted_iota(jnp.int32, (local_beads, LANES), 1)
    turned[...] = cycle_table(
        lane_j.astype(jnp.float32), (first + sub_b).astype(jnp.float32), beads
    )

    row_id = lax.broadcasted_iota(jnp.int32, (ROWS, LANES), 0)
    second = jnp.where(row_id < ROWS - REACH, row_id, row_id - ROWS).astype(jnp.float32)
    third = (row_id - REACH).astype(jnp.float32)

    for n in range(chunks):
        for copy in part_copies[n * (nb - 1) : (n + 1) * (nb - 1)]:
            copy.wait()
        total = part[me, n]
        for d in range(1, nb):
            total = total + land[d, n]
        site[n] = total - jnp.round(total)

        def build(t, carry, n=n):
            where = pl.ds(pl.multiple_of((n * span + t) * LANES, LANES), LANES)
            x = site[n, pl.ds(t, 1), :]
            step_r = jnp.broadcast_to(cos_turns(x), (ROWS, LANES))
            step_i = jnp.broadcast_to(sin_turns(x), (ROWS, LANES))
            y = second * site[n, pl.ds(span + t, 1), :]
            z = third * site[n, pl.ds(2 * span + t, 1), :]
            real, imag = cos_turns(y), sin_turns(y)
            reals, imags = [real[:HALF]], [imag[:HALF]]
            for a in range(REACH):
                real, imag = real * step_r - imag * step_i, real * step_i + imag * step_r
                reals.append(real)
                imags.append(imag)
            for base, parts in ((0, reals), (GRID, imags)):
                blocks = [parts[0]]
                for a in range(1, REACH + 1, 2):
                    blocks.append(jnp.concatenate(parts[a : a + 2], axis=0))
                at = base
                for block in blocks:
                    high, low = split(block)
                    xy_high[at : at + block.shape[0], where] = high
                    xy_low[at : at + block.shape[0], where] = low
                    at += block.shape[0]
            cos_z, sin_z = cos_turns(z), sin_turns(z)
            z_wave[0, :, where] = cos_z
            z_wave[1, :, where] = sin_z
            q_row = charge[chunk, pl.ds(n * span + t, 1), :]
            qc, qs = q_row * cos_z, q_row * sin_z
            for i, block in enumerate(((qc, qs), (-qs, qc))):
                high, low = split(jnp.concatenate(block, axis=0))
                z_mat[i, 0 : 2 * ROWS, where] = high
                z_mat[i, 2 * ROWS : 4 * ROWS, where] = low
            return carry

        lax.fori_loop(0, span, build, 0)

    pieces = factor_land.shape[1]
    count_tiles = 2 * ROWS * GRID // (8 * LANES)
    product = dot_nt(z_mat[0], xy_high[0:GRID, :]) + dot_nt(z_mat[1], xy_high[GRID : 2 * GRID, :])
    own = product[: 2 * ROWS] + product[2 * ROWS :]
    own = own + dot_nt(z_mat[0, 0 : 2 * ROWS, :], xy_low[0:GRID, :])
    own = own + dot_nt(z_mat[1, 0 : 2 * ROWS, :], xy_low[GRID : 2 * GRID, :])
    for l in range(GRID // LANES):
        for i in range(2 * ROWS // 8):
            factor[l * (2 * ROWS // 8) + i] = own[8 * i : 8 * i + 8, l * LANES : (l + 1) * LANES]
    for i in range(count_tiles, group * pieces):
        factor[i] = jnp.zeros((8, LANES), jnp.float32)
    factor_copies = []
    for d in range(1, group):
        peer = group_peer(d)
        target = peer[1] * share + lax.rem(peer[0], share)
        copy = pltpu.make_async_remote_copy(
            src_ref=factor.at[pl.ds(target * pieces, pieces)], dst_ref=factor_land.at[d],
            send_sem=send_fac.at[d], recv_sem=recv_fac.at[d], device_id=peer, device_id_type=MESH,
        )
        copy.start()
        factor_copies.append(copy)

    for copy in wave_copies:
        copy.wait()
    count = jnp.zeros((ROWS, GRID), jnp.float32)
    pair_id = lax.broadcasted_iota(jnp.int32, (GRID, kvec), 0).astype(jnp.float32)
    third_id = lax.broadcasted_iota(jnp.int32, (ROWS, kvec), 0).astype(jnp.float32)
    for n in range(nb):
        m = waves[n]
        m0, m1, m2 = m[0:1], m[1:2], m[2:3]
        wrapped = jnp.where(m1 < 0.0, m1 + ROWS, m1)
        pair = jnp.where(m0 > 0.0, HALF + (m0 - 1.0) * ROWS + wrapped, m1)
        hot_pair = jnp.where(pair_id == pair, 1.0, 0.0).astype(jnp.bfloat16)
        hot_third = jnp.where(third_id == m2 + REACH, 1.0, 0.0).astype(jnp.bfloat16)
        count = count + dot_nt(hot_third, hot_pair)

    mine = pl.ds(place * pieces, pieces)
    all_copies = []
    for copy in factor_copies:
        copy.wait()
    total = factor[mine]
    for d in range(1, group):
        total = total + factor_land[d]
    whole[mine] = total
    for d in range(1, group):
        copy = pltpu.make_async_remote_copy(
            src_ref=whole.at[mine], dst_ref=whole.at[mine], send_sem=send_all.at[d],
            recv_sem=recv_all.at[d], device_id=group_peer(d), device_id_type=MESH,
        )
        copy.start()
        all_copies.append(copy)

    col = lax.broadcasted_iota(jnp.int32, (ROWS, GRID), 1)
    line = lax.broadcasted_iota(jnp.int32, (ROWS, GRID), 0)
    f0 = jnp.zeros((ROWS, GRID), jnp.int32)
    for a in range(REACH):
        f0 = f0 + jnp.where(col >= HALF + a * ROWS, 1, 0)
    f1 = jnp.where(f0 > 0, col - HALF - (f0 - 1) * ROWS, col)
    f1 = jnp.where(f1 < ROWS - REACH, f1, f1 - ROWS)
    f2 = line - REACH
    f0, f1, f2 = f0.astype(jnp.float32), f1.astype(jnp.float32), f2.astype(jnp.float32)
    msq = f0 * f0 + f1 * f1 + f2 * f2
    weight = 4.0 * jnp.exp(-msq / 100.0) / (jnp.maximum(msq, 1.0) * float(sites * na))
    weight = weight * count
    w0, w1 = jnp.concatenate([f0, f0], axis=1), jnp.concatenate([f1, f1], axis=1)

    for copy in all_copies:
        copy.wait()
    per_lane = 2 * ROWS // 8
    half = per_lane // 2

    def gather(base):
        return jnp.concatenate(
            [
                jnp.concatenate([whole[l * per_lane + base + i] for i in range(half)], axis=0)
                for l in range(GRID // LANES)
            ],
            axis=1,
        )

    gr, gi = weight * gather(0), weight * gather(half)
    u, v = jnp.concatenate([-gi, gr], axis=1), jnp.concatenate([gr, gi], axis=1)
    left = jnp.concatenate([u, v, w0 * u, w0 * v, w1 * u, w1 * v], axis=0)
    left_high, left_low = split(left)
    left_both = jnp.concatenate([left_high, left_low], axis=0)
    height = 6 * ROWS

    width = 2 * LANES if span % 2 == 0 else LANES
    per = width // LANES
    m2_rows = (lax.broadcasted_iota(jnp.int32, (ROWS, width), 0) - REACH).astype(jnp.float32)
    force_copies = []
    for n in range(chunks):
        for k in range(span // per):
            start = (n * span + k * per) * LANES
            where = slice(start, start + width)
            both = dot_nn(left_both, xy_high[:, where])
            term = both[:height] + both[height:] + dot_nn(left_high, xy_low[:, where])
            cz, sz = z_wave[0, :, where], z_wave[1, :, where]
            blocks = [
                term[2 * i * ROWS : (2 * i + 1) * ROWS] * cz
                + term[(2 * i + 1) * ROWS : (2 * i + 2) * ROWS] * sz
                for i in range(3)
            ]
            along = (blocks[1], blocks[2], blocks[0] * m2_rows)
            for x in range(3):
                summed = TWO_PI * jnp.sum(along[x], axis=0, keepdims=True)
                for p in range(per):
                    t = k * per + p
                    q_row = charge[chunk, n * span + t : n * span + t + 1, :]
                    force[me, n, x * span + t : x * span + t + 1, :] = (
                        q_row * summed[:, p * LANES : (p + 1) * LANES]
                    )
        for d in range(1, nb):
            copy = pltpu.make_async_remote_copy(
                src_ref=force.at[me, n], dst_ref=force.at[me, n], send_sem=send_force.at[n, d],
                recv_sem=recv_force.at[n, d], device_id=bead_peer(d), device_id_type=MESH,
            )
            copy.start()
            force_copies.append(copy)

    table = turned[...]
    spread = [jnp.broadcast_to(table[:, j : j + 1], (local_beads, LANES)) for j in range(CONTR)]
    out_copies = []
    for n in range(chunks):
        for copy in force_copies[n * (nb - 1) : (n + 1) * (nb - 1)]:
            copy.wait()
        for c in range(share):
            for x in range(3):
                for t in range(span):
                    total = None
                    for j in range(CONTR):
                        row = x * span + t
                        term = spread[j] * force[j * share + c, n, row : row + 1, :]
                        total = term if total is None else total + term
                    at = (c * tiles + n * span + t) * LANES
                    out_ref[x, :, at : at + LANES] = total
            where = pl.ds((c * tiles + n * span) * LANES, span * LANES)
            copy = pltpu.make_async_copy(
                out_ref.at[:, :, where], out_hbm.at[:, :, where], out_sem.at[n * share + c]
            )
            copy.start()
            out_copies.append(copy)
    for copy in out_copies:
        copy.wait()


def local(nb, na, positions, waves, labels, values):
    local_beads, _, sites = positions.shape
    kvec = waves.shape[1]
    share = nb // CONTR
    own_sites = sites // share
    tiles = own_sites // LANES
    span = max(n for n in (1, 2, 3, 4) if tiles % n == 0)
    chunks = tiles // span
    rows = -(-3 * span // 8) * 8
    group = na * share
    pieces = -(-(2 * ROWS * GRID // (8 * LANES)) // group)
    dma = pltpu.SemaphoreType.DMA
    f32, bf16 = jnp.float32, jnp.bfloat16
    hbm = pl.BlockSpec(memory_space=pltpu.HBM)
    out = pl.pallas_call(
        functools.partial(kernel, nb, na),
        out_shape=jax.ShapeDtypeStruct((3, local_beads, sites), f32),
        in_specs=[hbm] * 4,
        out_specs=hbm,
        scratch_shapes=[
            pltpu.VMEM((3, local_beads, sites), f32),
            pltpu.SMEM(values.shape, f32),
            pltpu.VMEM((3, local_beads, sites), f32),
            pltpu.VMEM((3, kvec), jnp.int32),
            pltpu.VMEM((sites // LANES, LANES), jnp.int32),
            pltpu.VMEM((nb, chunks, rows, LANES), f32),
            pltpu.VMEM((nb, chunks, rows, LANES), f32),
            pltpu.VMEM((chunks, rows, LANES), f32),
            pltpu.VMEM((nb, 8, kvec), f32),
            pltpu.VMEM((share, -(-tiles // 8) * 8, LANES), f32),
            pltpu.VMEM((2 * GRID, own_sites), bf16),
            pltpu.VMEM((2 * GRID, own_sites), bf16),
            pltpu.VMEM((2, 4 * ROWS, own_sites), bf16),
            pltpu.VMEM((2, ROWS, own_sites), f32),
            pltpu.VMEM((group * pieces, 8, LANES), f32),
            pltpu.VMEM((group, pieces, 8, LANES), f32),
            pltpu.VMEM((group * pieces, 8, LANES), f32),
            pltpu.VMEM((local_beads, LANES), f32),
            pltpu.VMEM((nb, chunks, rows, LANES), f32),
            dma((3,)), dma((chunks * share,)), dma((chunks * share,)), dma((nb,)), dma((nb,)), dma((chunks, nb)), dma((chunks, nb)),
            dma((group,)), dma((group,)), dma((group,)), dma((group,)), dma((chunks, nb)), dma((chunks, nb)),
        ],
        compiler_params=pltpu.CompilerParams(
            collective_id=0, has_side_effects=True, vmem_limit_bytes=60 * 1024 * 1024
        ),
    )(values, jnp.transpose(positions, (1, 0, 2)), waves, labels.reshape(-1, LANES))
    return jnp.transpose(out, (1, 0, 2))


def solution(mesh):
    in_specs = (P("bead", None, "atom"), P(None, "bead"), P("atom"), P())
    out_specs = P("bead", None, "atom")
    body = functools.partial(local, mesh.shape["bead"], mesh.shape["atom"])
    return jax.shard_map(body, mesh=mesh, in_specs=in_specs, out_specs=out_specs, check_vma=False)
```

time: 28.3 us -> 28.2 us (level)
  local copies, waits for them, and re-layouts: 3.71 us -> 1.69 us
  Pallas kernels: 24.4 us -> 26.3 us
    unnamed x9 -> x1, local copies, waits for them, and re-layouts: 3.71 us -> 1.69 us
    pallas_call x1, Pallas kernels: 24.4 us -> 26.3 us  [local(): pl.pallas_call(functools.partial(kernel, nb, na), out_shape=jax.ShapeDtyp...]
where the time goes in v2:
time: 28.2 us; the launch traced here: 28 us
  Pallas kernels  26.3 us (93%)
  local copies, waits for them, and re-layouts  1.69 us (6%)
    pallas_call x1, Pallas kernels, local(): pl.pallas_call(functools.partial(kernel, nb, na), out_shape=jax.ShapeDtyp...  26.3 us
    unnamed x1, local copies, waits for them, and re-layouts  1.69 us

profile of v2, /device:TPU:0, one launch (start us, length us, event | category | flops | bytes accessed | tf_op | source)
XLA Modules:
  0.0 28.0 jit_solution(7442233028349987887)
XLA Ops:
  0.0 26.3 %shard_map.46 = f32[3,16,1536]{2,1,0:T(8,128)} custom-call(f32[4]{0:T(128)} %values_hbm.1, f32[3,16,1536]{2,1,0:T(8,128)} %bitcast.4, s32[3,256]{1,0:T(4,128)} %wave_hbm.1, s32[12,128]{1,0:T(8,128)} %bitcast.5), custom_call_target="tpu_custom_call" | custom-call | tf_op jit(solution)/shard_map/pallas_call | solution.py:384
  26.3 1.7 %copy.6 = f32[16,3,1536]{2,0,1:T(8,128)} copy(f32[16,3,1536]{2,0,1:T(8,128)} %bitcast.3) | data formatting | bytes 589824

commit v3 on v2

--- a/solution.py
+++ b/solution.py
@@ -68,10 +68,10 @@
 
 
 def kernel(
-    nb, na, values_hbm, pos_hbm, wave_hbm, label_hbm, out_hbm,
-    out_ref, values, pos, wave_in, label_in,
-    part, land, site, waves, charge, xy_high, xy_low, z_mat, z_wave, factor, factor_land, whole, turned, force,
-    in_sem, pos_sem, out_sem, send_wave, recv_wave, send_part, recv_part, send_fac, recv_fac, send_all, recv_all,
+    nb, na, values_hbm, pos_hbm, wave_hbm, label_hbm, gathered,
+    values, pos, wave_in, label_in,
+    part, land, site, waves, charge, xy_high, xy_low, z_mat, z_wave, factor, factor_land, whole, force,
+    in_sem, pos_sem, send_wave, recv_wave, send_part, recv_part, send_fac, recv_fac,
     send_force, recv_force,
 ):
     share = nb // CONTR
@@ -143,6 +143,13 @@
                         part[j * share + c, n, row : row + 1, :] = total[j : j + 1, :]
         if n == 0:
             pl.semaphore_wait(barrier, len(peers))
+            for d in range(1, nb):
+                copy = pltpu.make_async_remote_copy(
+                    src_ref=waves.at[me], dst_ref=waves.at[me], send_sem=send_wave.at[d],
+                    recv_sem=recv_wave.at[d], device_id=bead_peer(d), device_id_type=MESH,
+                )
+                copy.start()
+                wave_copies.append(copy)
         for d in range(1, nb):
             peer = bead_peer(d)
             copy = pltpu.make_async_remote_copy(
@@ -151,14 +158,6 @@
             )
             copy.start()
             part_copies.append(copy)
-    for d in range(1, nb):
-        copy = pltpu.make_async_remote_copy(
-            src_ref=waves.at[me], dst_ref=waves.at[me], send_sem=send_wave.at[d],
-            recv_sem=recv_wave.at[d], device_id=bead_peer(d), device_id_type=MESH,
-        )
-        copy.start()
-        wave_copies.append(copy)
-
     label_copy.wait()
     value_copy.wait()
     label = label_in[...]
@@ -167,11 +166,6 @@
         q = q + jnp.where(label == kind, values[kind], 0.0)
     for c in range(share):
         charge[c, 0:tiles, :] = q[c * tiles : (c + 1) * tiles, :]
-    sub_b = lax.broadcasted_iota(jnp.int32, (local_beads, LANES), 0)
-    lane_j = lax.broadcasted_iota(jnp.int32, (local_beads, LANES), 1)
-    turned[...] = cycle_table(
-        lane_j.astype(jnp.float32), (first + sub_b).astype(jnp.float32), beads
-    )
 
     row_id = lax.broadcasted_iota(jnp.int32, (ROWS, LANES), 0)
     second = jnp.where(row_id < ROWS - REACH, row_id, row_id - ROWS).astype(jnp.float32)
@@ -221,7 +215,7 @@
 
         lax.fori_loop(0, span, build, 0)
 
-    pieces = factor_land.shape[1]
+    pieces = factor_land.shape[1] // group
     count_tiles = 2 * ROWS * GRID // (8 * LANES)
     product = dot_nt(z_mat[0], xy_high[0:GRID, :]) + dot_nt(z_mat[1], xy_high[GRID : 2 * GRID, :])
     own = product[: 2 * ROWS] + product[2 * ROWS :]
@@ -237,7 +231,7 @@
         peer = group_peer(d)
         target = peer[1] * share + lax.rem(peer[0], share)
         copy = pltpu.make_async_remote_copy(
-            src_ref=factor.at[pl.ds(target * pieces, pieces)], dst_ref=factor_land.at[d],
+            src_ref=factor, dst_ref=factor_land.at[d],
             send_sem=send_fac.at[d], recv_sem=recv_fac.at[d], device_id=peer, device_id_type=MESH,
         )
         copy.start()
@@ -257,21 +251,13 @@
         hot_third = jnp.where(third_id == m2 + REACH, 1.0, 0.0).astype(jnp.bfloat16)
         count = count + dot_nt(hot_third, hot_pair)
 
-    mine = pl.ds(place * pieces, pieces)
-    all_copies = []
+
     for copy in factor_copies:
         copy.wait()
-    total = factor[mine]
+    total = factor[...]
     for d in range(1, group):
         total = total + factor_land[d]
-    whole[mine] = total
-    for d in range(1, group):
-        copy = pltpu.make_async_remote_copy(
-            src_ref=whole.at[mine], dst_ref=whole.at[mine], send_sem=send_all.at[d],
-            recv_sem=recv_all.at[d], device_id=group_peer(d), device_id_type=MESH,
-        )
-        copy.start()
-        all_copies.append(copy)
+    whole[...] = total
 
     col = lax.broadcasted_iota(jnp.int32, (ROWS, GRID), 1)
     line = lax.broadcasted_iota(jnp.int32, (ROWS, GRID), 0)
@@ -287,8 +273,6 @@
     weight = weight * count
     w0, w1 = jnp.concatenate([f0, f0], axis=1), jnp.concatenate([f1, f1], axis=1)
 
-    for copy in all_copies:
-        copy.wait()
     per_lane = 2 * ROWS // 8
     half = per_lane // 2
 
@@ -330,40 +314,55 @@
                 for p in range(per):
                     t = k * per + p
                     q_row = charge[chunk, n * span + t : n * span + t + 1, :]
-                    force[me, n, x * span + t : x * span + t + 1, :] = (
+                    force[n, x * span + t : x * span + t + 1, :] = (
                         q_row * summed[:, p * LANES : (p + 1) * LANES]
                     )
         for d in range(1, nb):
             copy = pltpu.make_async_remote_copy(
-                src_ref=force.at[me, n], dst_ref=force.at[me, n], send_sem=send_force.at[n, d],
+                src_ref=force.at[n], dst_ref=gathered.at[me, n], send_sem=send_force.at[n, d],
                 recv_sem=recv_force.at[n, d], device_id=bead_peer(d), device_id_type=MESH,
             )
             copy.start()
             force_copies.append(copy)
 
-    table = turned[...]
+    own_copy = pltpu.make_async_copy(force, gathered.at[me], in_sem.at[3])
+    own_copy.start()
+    for copy in force_copies:
+        copy.wait()
+    own_copy.wait()
+
+
+def expand(nb, force_hbm, out_hbm, force, out, in_sem, out_sem):
+    share = nb // CONTR
+    chunks = force.shape[1]
+    local_beads, sites = out.shape[1], out.shape[2]
+    tiles = sites // share // LANES
+    span = tiles // chunks
+    copy_in = pltpu.make_async_copy(force_hbm, force, in_sem)
+    copy_in.start()
+    first = lax.axis_index("bead") * local_beads
+    sub = lax.broadcasted_iota(jnp.int32, (local_beads, LANES), 0)
+    lane = lax.broadcasted_iota(jnp.int32, (local_beads, LANES), 1)
+    table = cycle_table(
+        lane.astype(jnp.float32), (first + sub).astype(jnp.float32), local_beads * nb
+    )
     spread = [jnp.broadcast_to(table[:, j : j + 1], (local_beads, LANES)) for j in range(CONTR)]
-    out_copies = []
-    for n in range(chunks):
-        for copy in force_copies[n * (nb - 1) : (n + 1) * (nb - 1)]:
-            copy.wait()
+    copy_in.wait()
+    copies = []
+    for x in range(3):
         for c in range(share):
-            for x in range(3):
-                for t in range(span):
-                    total = None
-                    for j in range(CONTR):
-                        row = x * span + t
-                        term = spread[j] * force[j * share + c, n, row : row + 1, :]
-                        total = term if total is None else total + term
-                    at = (c * tiles + n * span + t) * LANES
-                    out_ref[x, :, at : at + LANES] = total
-            where = pl.ds((c * tiles + n * span) * LANES, span * LANES)
-            copy = pltpu.make_async_copy(
-                out_ref.at[:, :, where], out_hbm.at[:, :, where], out_sem.at[n * share + c]
-            )
-            copy.start()
-            out_copies.append(copy)
-    for copy in out_copies:
+            for t in range(tiles):
+                total = None
+                for j in range(CONTR):
+                    row = x * span + t % span
+                    term = spread[j] * force[j * share + c, t // span, row : row + 1, :]
+                    total = term if total is None else total + term
+                at = (c * tiles + t) * LANES
+                out[x, :, at : at + LANES] = total
+        copy = pltpu.make_async_copy(out.at[x], out_hbm.at[x], out_sem.at[x])
+        copy.start()
+        copies.append(copy)
+    for copy in copies:
         copy.wait()
 
 
@@ -373,7 +372,7 @@
     share = nb // CONTR
     own_sites = sites // share
     tiles = own_sites // LANES
-    span = max(n for n in (1, 2, 3, 4) if tiles % n == 0)
+    span = tiles
     chunks = tiles // span
     rows = -(-3 * span // 8) * 8
     group = na * share
@@ -381,13 +380,12 @@
     dma = pltpu.SemaphoreType.DMA
     f32, bf16 = jnp.float32, jnp.bfloat16
     hbm = pl.BlockSpec(memory_space=pltpu.HBM)
-    out = pl.pallas_call(
+    gathered = pl.pallas_call(
         functools.partial(kernel, nb, na),
-        out_shape=jax.ShapeDtypeStruct((3, local_beads, sites), f32),
+        out_shape=jax.ShapeDtypeStruct((nb, chunks, rows, LANES), f32),
         in_specs=[hbm] * 4,
         out_specs=hbm,
         scratch_shapes=[
-            pltpu.VMEM((3, local_beads, sites), f32),
             pltpu.SMEM(values.shape, f32),
             pltpu.VMEM((3, local_beads, sites), f32),
             pltpu.VMEM((3, kvec), jnp.int32),
@@ -402,17 +400,28 @@
             pltpu.VMEM((2, 4 * ROWS, own_sites), bf16),
             pltpu.VMEM((2, ROWS, own_sites), f32),
             pltpu.VMEM((group * pieces, 8, LANES), f32),
-            pltpu.VMEM((group, pieces, 8, LANES), f32),
+            pltpu.VMEM((group, group * pieces, 8, LANES), f32),
             pltpu.VMEM((group * pieces, 8, LANES), f32),
-            pltpu.VMEM((local_beads, LANES), f32),
-            pltpu.VMEM((nb, chunks, rows, LANES), f32),
-            dma((3,)), dma((chunks * share,)), dma((chunks * share,)), dma((nb,)), dma((nb,)), dma((chunks, nb)), dma((chunks, nb)),
-            dma((group,)), dma((group,)), dma((group,)), dma((group,)), dma((chunks, nb)), dma((chunks, nb)),
+            pltpu.VMEM((chunks, rows, LANES), f32),
+            dma((4,)), dma((chunks * share,)), dma((nb,)), dma((nb,)), dma((chunks, nb)), dma((chunks, nb)),
+            dma((group,)), dma((group,)), dma((chunks, nb)), dma((chunks, nb)),
         ],
         compiler_params=pltpu.CompilerParams(
             collective_id=0, has_side_effects=True, vmem_limit_bytes=60 * 1024 * 1024
         ),
     )(values, jnp.transpose(positions, (1, 0, 2)), waves, labels.reshape(-1, LANES))
+    out = pl.pallas_call(
+        functools.partial(expand, nb),
+        out_shape=jax.ShapeDtypeStruct((3, local_beads, sites), f32),
+        in_specs=[hbm],
+        out_specs=hbm,
+        scratch_shapes=[
+            pltpu.VMEM((nb, chunks, rows, LANES), f32),
+            pltpu.VMEM((3, local_beads, sites), f32),
+            dma, dma((3,)),
+        ],
+        compiler_params=pltpu.CompilerParams(vmem_limit_bytes=60 * 1024 * 1024),
+    )(gathered)
     return jnp.transpose(out, (1, 0, 2))
 
 

time: 28.2 us -> 26.1 us (0.926)
  local copies, waits for them, and re-layouts: 1.69 us -> 0 us
  Pallas kernels: 26.3 us -> 26 us
    pallas_call x1, Pallas kernels: 26.3 us -> 24.2 us  [local(): pl.pallas_call(functools.partial(kernel, nb, na), out_shape=jax.ShapeDtyp...]
    pallas_call x0 -> x1, Pallas kernels: none -> 1.74 us  [local(): pl.pallas_call(functools.partial(expand, nb), out_shape=jax.ShapeDtypeStr...]
    unnamed x1 -> x0, local copies, waits for them, and re-layouts: 1.69 us -> none
where the time goes in v3:
time: 26.1 us; the launch traced here: 26 us
  Pallas kernels  26 us (100%)
    pallas_call x1, Pallas kernels, local(): pl.pallas_call(functools.partial(kernel, nb, na), out_shape=jax.ShapeDtyp...  24.2 us
    pallas_call x1, Pallas kernels, local(): pl.pallas_call(functools.partial(expand, nb), out_shape=jax.ShapeDtypeStr...  1.74 us

profile of v3, /device:TPU:0, one launch (start us, length us, event | category | flops | bytes accessed | tf_op | source)
XLA Modules:
  0.0 26.0 jit_solution(9851073472460159369)
XLA Ops:
  0.0 24.2 %shard_map.46.force_hbm = f32[8,1,40,128]{3,2,1,0:T(8,128)} custom-call(f32[4]{0:T(128)} %values_hbm.1, f32[3,16,1536]{2,1,0:T(8,128)} %bitcast.3, s32[3,256]{1,0:T(4,128)} %wave_hbm.1, s32[12,128]{1,0:T(8,128)} %bitcast.4), custom_call_target="tpu_custom_call" | custom-call | tf_op jit(solution)/shard_map/pallas_call | solution.py:383
  24.2 1.7 %shard_map.47 = f32[3,16,1536]{2,1,0:T(8,128)} custom-call(f32[8,1,40,128]{3,2,1,0:T(8,128)} %shard_map.46.force_hbm), custom_call_target="tpu_custom_call" | custom-call | tf_op jit(solution)/shard_map/pallas_call | solution.py:413

commit v4 on v3

--- a/solution.py
+++ b/solution.py
@@ -251,14 +251,6 @@
         hot_third = jnp.where(third_id == m2 + REACH, 1.0, 0.0).astype(jnp.bfloat16)
         count = count + dot_nt(hot_third, hot_pair)
 
-
-    for copy in factor_copies:
-        copy.wait()
-    total = factor[...]
-    for d in range(1, group):
-        total = total + factor_land[d]
-    whole[...] = total
-
     col = lax.broadcasted_iota(jnp.int32, (ROWS, GRID), 1)
     line = lax.broadcasted_iota(jnp.int32, (ROWS, GRID), 0)
     f0 = jnp.zeros((ROWS, GRID), jnp.int32)
@@ -272,6 +264,13 @@
     weight = 4.0 * jnp.exp(-msq / 100.0) / (jnp.maximum(msq, 1.0) * float(sites * na))
     weight = weight * count
     w0, w1 = jnp.concatenate([f0, f0], axis=1), jnp.concatenate([f1, f1], axis=1)
+
+    for copy in factor_copies:
+        copy.wait()
+    total = factor[...]
+    for d in range(1, group):
+        total = total + factor_land[d]
+    whole[...] = total
 
     per_lane = 2 * ROWS // 8
     half = per_lane // 2

time: 26.1 us -> 26.1 us (level)
  no operation moved by 1% of the time
where the time goes in v4:
time: 26.1 us; the launch traced here: 26 us
  Pallas kernels  26 us (100%)
    pallas_call x1, Pallas kernels, local(): pl.pallas_call(functools.partial(kernel, nb, na), out_shape=jax.ShapeDtyp...  24.2 us
    pallas_call x1, Pallas kernels, local(): pl.pallas_call(functools.partial(expand, nb), out_shape=jax.ShapeDtypeStr...  1.74 us

profile of v4, /device:TPU:0, one launch (start us, length us, event | category | flops | bytes accessed | tf_op | source)
XLA Modules:
  0.0 26.0 jit_solution(12797427650095259181)
XLA Ops:
  0.0 24.2 %shard_map.46.force_hbm = f32[8,1,40,128]{3,2,1,0:T(8,128)} custom-call(f32[4]{0:T(128)} %values_hbm.1, f32[3,16,1536]{2,1,0:T(8,128)} %bitcast.3, s32[3,256]{1,0:T(4,128)} %wave_hbm.1, s32[12,128]{1,0:T(8,128)} %bitcast.4), custom_call_target="tpu_custom_call" | custom-call | tf_op jit(solution)/shard_map/pallas_call | solution.py:382
  24.2 1.7 %shard_map.47 = f32[3,16,1536]{2,1,0:T(8,128)} custom-call(f32[8,1,40,128]{3,2,1,0:T(8,128)} %shard_map.46.force_hbm), custom_call_target="tpu_custom_call" | custom-call | tf_op jit(solution)/shard_map/pallas_call | solution.py:412
